TPU v7x, 128 devices: a whole 4x4x4 slice. The times are simulated.
128 devices in a mesh: pipe: 4 (over z_lo, core), dp: 32 (over x, z_hi, y).
Axes of the slice: x: 4, y: 4, z: 4 (z_hi: 2, z_lo: 2; z = z_hi * 2 + z_lo), core: 2. Of those that a mesh axis runs over, the one named last changes fastest.
Arguments:
- segment_data: bfloat16 [4, 32, 2, 512, 384], P('pipe', 'dp'), may hold values from -6 to 6
- clip_frames: int32 [32, 2, 2, 8], P('dp'), may hold values from 0 to 32, as said below
- encoder_gains: bfloat16 [2, 384], replicated, may hold values from 0.25 to 1.75
- encoder_biases: bfloat16 [6, 384], replicated, may hold values from -3 to 3
- encoder_project: bfloat16 [384, 1152], replicated, may hold values from -0.3125 to 0.3125
- encoder_merge: bfloat16 [384, 384], replicated, may hold values from -1.25 to 1.25
- encoder_expand: bfloat16 [384, 1536], replicated, may hold values from -0.3125 to 0.3125
- encoder_expand_bias: bfloat16 [1536], replicated, may hold values from -3 to 3
- encoder_reduce: bfloat16 [1536, 384], replicated, may hold values from -0.15625 to 0.15625
- predictor_embed: bfloat16 [384, 384], replicated, may hold values from -0.3125 to 0.3125
- predictor_embed_bias: bfloat16 [384], replicated, may hold values from -3 to 3
- predictor_gains: bfloat16 [2, 384], replicated, may hold values from 0.25 to 1.75
- predictor_biases: bfloat16 [6, 384], replicated, may hold values from -3 to 3
- predictor_project: bfloat16 [384, 1152], replicated, may hold values from -0.3125 to 0.3125
- predictor_merge: bfloat16 [384, 384], replicated, may hold values from -1.25 to 1.25
- predictor_expand: bfloat16 [384, 1536], replicated, may hold values from -0.3125 to 0.3125
- predictor_expand_bias: bfloat16 [1536], replicated, may hold values from -3 to 3
- predictor_reduce: bfloat16 [1536, 384], replicated, may hold values from -0.15625 to 0.15625
Outputs:
- segment_result: float32 [4, 32, 2, 512, 384], P('pipe', 'dp')
- grad_encoder_gains: float32 [2, 384], replicated
- grad_encoder_biases: float32 [6, 384], replicated
- grad_encoder_project: float32 [384, 1152], replicated
- grad_encoder_merge: float32 [384, 384], replicated
- grad_encoder_expand: float32 [384, 1536], replicated
- grad_encoder_expand_bias: float32 [1536], replicated
- grad_encoder_reduce: float32 [1536, 384], replicated
- grad_predictor_embed: float32 [384, 384], replicated
- grad_predictor_embed_bias: float32 [384], replicated
- grad_predictor_gains: float32 [2, 384], replicated
- grad_predictor_biases: float32 [6, 384], replicated
- grad_predictor_project: float32 [384, 1152], replicated
- grad_predictor_merge: float32 [384, 384], replicated
- grad_predictor_expand: float32 [384, 1536], replicated
- grad_predictor_expand_bias: float32 [1536], replicated
- grad_predictor_reduce: float32 [1536, 384], replicated
Inputs may be any that keep to these rules, and one draw needn't show every extreme that they name: `clip_frames`: in each slot the nonzero counts (8, 16 or 32) come first and zeros after; every slot holds at least one clip; a slot's counts sum to at most 64, and some slot reaches that sum in every draw.
All inputs are finite; a program needn't handle non-finite values.
Results may differ from a plain program's by a relative error of at most 0.025.
Values may be sent and summed in bfloat16 or wider, within the bound.
A program may use at most 256 MiB of HBM per device.

v0:
```python
import functools
import math

import jax
import jax.numpy as jnp
from jax import lax
from jax.experimental import pallas as pl
from jax.experimental.pallas import tpu as pltpu
from jax.sharding import PartitionSpec as P

HEADS = 6
PHEADS = 12
CLIPS = 8
F = 384
FF = 1536
ROWS = 512
UNIT = 64
UNITS = ROWS // UNIT
BLOCK = 256
BLOCKS = ROWS // BLOCK
TOTAL = 10240
EPS = 1e-06
MASKED = -1e30

f32 = jnp.float32
bf16 = jnp.bfloat16


def dot(a, b, ca, cb):
    return lax.dot_general(a, b, (((ca,), (cb,)), ((), ())), preferred_element_type=f32)


def unit_order(frames):
    rows = [frames[c] * (UNIT // 8) for c in range(CLIPS)]
    start, place = [], []
    total = jnp.int32(0)
    for c in range(CLIPS):
        start.append(total)
        total = total + rows[c]
    for c in range(CLIPS):
        before = jnp.int32(0)
        for d in range(CLIPS):
            if d < c:
                ahead = rows[d] >= rows[c]
            elif d > c:
                ahead = rows[d] > rows[c]
            else:
                continue
            before = before + jnp.where(ahead, rows[d], 0)
        place.append(before)
    source, label = [], []
    for j in range(UNITS):
        at = j * UNIT
        src, lab = jnp.int32(at), jnp.int32(CLIPS + j)
        for c in range(CLIPS):
            held = (at >= place[c]) & (at < place[c] + rows[c])
            src = jnp.where(held, start[c] + at - place[c], src)
            lab = jnp.where(held, c, lab)
        source.append(src)
        label.append(lab)
    return source, label, total


def fill_order(order_ref, source):
    lane = lax.broadcasted_iota(jnp.int32, (1, ROWS), 1)
    row = spread(source, (1, ROWS), 1) + lane % UNIT
    at = lax.broadcasted_iota(jnp.int32, (ROWS, ROWS), 0)
    order_ref[...] = jnp.where(at == row, 1.0, 0.0).astype(bf16)


def spread(values, shape, axis):
    at = lax.broadcasted_iota(jnp.int32, shape, axis) // UNIT
    out = jnp.full(shape, values[0], jnp.int32)
    for i in range(1, len(values)):
        out = jnp.where(at == i, values[i], out)
    return out


def fill_mask(mask_ref, label):
    for b in range(BLOCKS):
        own = label[b * 4 : b * 4 + 4]
        down = spread(own, (BLOCK, BLOCK), 0)
        across = spread(own, (BLOCK, BLOCK), 1)
        mask_ref[b] = jnp.where(down == across, 0.0, MASKED).astype(f32)


def norm(v, gain, shift):
    mean = jnp.mean(v, axis=0, keepdims=True)
    centred = v - mean
    inverse = lax.rsqrt(jnp.mean(centred * centred, axis=0, keepdims=True) + EPS)
    normed = centred * inverse
    return normed * gain + shift, normed, inverse


def norm_back(k, normed, inverse):
    return inverse * (
        k
        - jnp.mean(k, axis=0, keepdims=True)
        - normed * jnp.mean(k * normed, axis=0, keepdims=True)
    )


def block_forward(stream_ref, out_ref, w, s, heads, mask_ref):
    size = F // heads
    scale = math.log2(math.e) / math.sqrt(size)
    vec = w.vec
    for t in range(ROWS // 128):
        cols = slice(t * 128, t * 128 + 128)
        full, normed, inverse = norm(stream_ref[:, cols], vec[:, 0:1], vec[:, 2:3])
        s.n1[:, cols] = normed
        s.i1[:, cols] = inverse
        s.a1[:, cols] = full.astype(bf16)
    for part in range(3):
        rows = slice(part * F, part * F + F)
        z = dot(w.project[:, rows], s.a1[...], 0, 0)
        if part == 0:
            z = z + vec[:, 3:4]
        if part == 2:
            z = z + vec[:, 4:5]
        s.z[rows, :] = z.astype(bf16)
    turns = [(h, b) for h in range(heads) for b in range(BLOCKS)]

    def place_of(h, b):
        return slice(h * size, h * size + size), slice(b * BLOCK, b * BLOCK + BLOCK)

    def score_of(h, b):
        own, cols = place_of(h, b)
        return dot(s.z[F + h * size : F + h * size + size, cols], s.z[own, cols], 0, 0)

    ahead = [score_of(*turn) for turn in turns[:3]]
    for i, (h, b) in enumerate(turns):
        own, cols = place_of(h, b)
        score = ahead.pop(0) * scale + mask_ref[b]
        if i + 3 < len(turns):
            ahead.append(score_of(*turns[i + 3]))
        e = jnp.exp2(score - jnp.max(score, axis=0, keepdims=True))
        over = 1.0 / jnp.sum(e, axis=0, keepdims=True)
        e = e.astype(bf16)
        s.e[h, b] = e
        s.over[h : h + 1, cols] = over
        v = s.z[2 * F + h * size : 2 * F + h * size + size, cols]
        s.o[own, cols] = (dot(v, e, 1, 0) * over).astype(bf16)
    middle = stream_ref[...] + (dot(w.merge[...], s.o[...], 0, 0) + vec[:, 5:6])
    s.m1[...] = middle
    for t in range(ROWS // 128):
        cols = slice(t * 128, t * 128 + 128)
        full, normed, inverse = norm(s.m1[:, cols], vec[:, 1:2], vec[:, 6:7])
        s.n2[:, cols] = normed
        s.i2[:, cols] = inverse
        s.a2[:, cols] = full.astype(bf16)
    for part in range(4):
        rows = slice(part * F, part * F + F)
        u = dot(w.expand[:, rows], s.a2[...], 0, 0) + vec[:, 8 + part : 9 + part]
        below = 0.5 * lax.erf(u * math.sqrt(0.5)) + 0.5
        density = jnp.exp2(u * u * (-0.5 * math.log2(math.e))) * (1.0 / math.sqrt(2.0 * math.pi))
        s.act[rows, :] = (u * below).astype(bf16)
        s.slope[rows, :] = (below + u * density).astype(bf16)
    out_ref[...] = s.m1[...] + (dot(w.reduce[...], s.act[...], 0, 0) + vec[:, 7:8])


def place(g_ref, at, value):
    for c in range(3):
        g_ref[c, at : at + value.shape[0], :] = value[:, c * 128 : c * 128 + 128].astype(bf16)


def total(x):
    return jnp.sum(x.astype(f32), axis=1, keepdims=True)


def block_backward(grad_ref, w, s, heads, g_ref, at, tick):
    size = F // heads
    vec = w.vec
    sums = [None] * 12
    s.q[...] = grad_ref[...].astype(bf16)
    q2 = s.q[...]
    sums[7] = total(q2)
    ahead = dot(w.reduce[0:F, :], q2, 1, 0)
    for part in range(4):
        rows = slice(part * F, part * F + F)
        grad_act = ahead
        if part < 3:
            ahead = dot(w.reduce[part * F + F : part * F + 2 * F, :], q2, 1, 0)
        du = (grad_act * s.slope[rows, :].astype(f32)).astype(bf16)
        s.du[rows, :] = du
        sums[8 + part] = total(du)
        place(g_ref, at["reduce"] + part * F, dot(s.act[rows, :], q2, 1, 1))
        tick()
    da = dot(w.expand[...], s.du[...], 1, 0)
    s.t[...] = da
    for t in range(ROWS // 128):
        cols = slice(t * 128, t * 128 + 128)
        grad_ref[:, cols] += norm_back(s.t[:, cols] * vec[:, 1:2], s.n2[:, cols], s.i2[:, cols])
        place(g_ref, at["expand"] + t * F, dot(s.a2[...], s.du[t * F : t * F + F, :], 1, 1))
    tick()
    sums[1] = total(s.t[...] * s.n2[...])
    sums[6] = total(s.t[...])
    s.q[...] = grad_ref[...].astype(bf16)
    q1 = s.q[...]
    sums[5] = total(q1)
    place(g_ref, at["merge"], dot(s.o[...], q1, 1, 1))
    s.t[...] = dot(w.merge[...], q1, 1, 0)
    tick()
    turns = [(h, b) for h in range(heads) for b in range(BLOCKS)]

    def slope_of(h, b):
        own, cols = slice(h * size, h * size + size), slice(b * BLOCK, b * BLOCK + BLOCK)
        do = (s.t[own, cols] * s.over[h : h + 1, cols]).astype(bf16)
        delta = jnp.sum(do.astype(f32) * s.o[own, cols].astype(f32), axis=0, keepdims=True)
        v = s.z[2 * F + h * size : 2 * F + h * size + size, cols]
        return do, delta, dot(v, do, 0, 0)

    ahead = [slope_of(*turn) for turn in turns[:2]]
    for i, (h, b) in enumerate(turns):
        cols = slice(b * BLOCK, b * BLOCK + BLOCK)
        lo = h * size
        q = s.z[lo : lo + size, cols]
        k = s.z[F + lo : F + lo + size, cols]
        do, delta, dp = ahead.pop(0)
        if i + 2 < len(turns):
            ahead.append(slope_of(*turns[i + 2]))
        e = s.e[h, b]
        ds = (dp - delta).astype(bf16) * e
        s.dz[2 * F + lo : 2 * F + lo + size, cols] = dot(do, e, 1, 1).astype(bf16)
        s.dz[lo : lo + size, cols] = (dot(k, ds, 1, 0) * (1.0 / math.sqrt(size))).astype(bf16)
        s.dz[F + lo : F + lo + size, cols] = (dot(q, ds, 1, 1) * (1.0 / math.sqrt(size))).astype(bf16)
        if i % 4 == 3:
            tick()
    sums[3] = total(s.dz[0:F, :])
    sums[4] = total(s.dz[2 * F : 3 * F, :])
    da = dot(w.project[...], s.dz[...], 1, 0)
    s.t[...] = da
    for t in range(ROWS // 128):
        cols = slice(t * 128, t * 128 + 128)
        grad_ref[:, cols] += norm_back(s.t[:, cols] * vec[:, 0:1], s.n1[:, cols], s.i1[:, cols])
        if t < 3:
            place(g_ref, at["project"] + t * F, dot(s.a1[...], s.dz[t * F : t * F + F, :], 1, 1))
    sums[0] = total(s.t[...] * s.n1[...])
    sums[2] = total(s.t[...])
    tick()
    return sums


def columns(gains, biases, hidden):
    rows = [gains.astype(f32), biases.astype(f32)]
    for part in range(4):
        rows.append(hidden[part * F : part * F + F].astype(f32).reshape(1, F))
    rows.append(jnp.zeros((4, F), f32))
    return jnp.concatenate(rows, axis=0).T


def place_sums(g_ref, at, sums):
    lane = lax.broadcasted_iota(jnp.int32, (F, 128), 1)
    table = jnp.zeros((F, 128), f32)
    for i, column in enumerate(sums):
        table = jnp.where(lane == i, column, table)
    place(g_ref, at, table.T[0:16, :])


class Refs:
    pass


KEPT = (
    ("n1", (F, ROWS), f32), ("i1", (1, ROWS), f32), ("a1", (F, ROWS), bf16), ("z", (3 * F, ROWS), bf16),
    ("o", (F, ROWS), bf16), ("m1", (F, ROWS), f32), ("n2", (F, ROWS), f32), ("i2", (1, ROWS), f32),
    ("a2", (F, ROWS), bf16), ("act", (FF, ROWS), bf16), ("slope", (FF, ROWS), bf16),
)
SHARED = (
    ("q", (F, ROWS), bf16), ("du", (FF, ROWS), bf16), ("t", (F, ROWS), f32), ("dz", (3 * F, ROWS), bf16),
)


PHASES = ((0, 3072, True, False), (3072, 2048, True, False), (5120, 1536, False, False), (6656, 2048, False, False), (8704, 1536, False, False))
PRED_AT = {"reduce": 0, "expand": 1536, "merge": 3072, "project": 3456, "embed": 4608, "small": 4992, "end": 5008}
ENC_AT = {"reduce": 5120, "expand": 6656, "merge": 8192, "gap": 8576, "project": 8704, "small": 9856, "end": 9872}
ORDERS = ("xyz", "yzx", "zxy")
WEIGHTS = (
    ("ew", (F, 3 * F)), ("em", (F, F)), ("ex", (F, FF)), ("er", (FF, F)), ("embed", (F, F)),
    ("pw", (F, 3 * F)), ("pm", (F, F)), ("px", (F, FF)), ("pr", (FF, F)),
)


class Where:
    def __init__(self):
        p, d = lax.axis_index("pipe"), lax.axis_index("dp")
        self.core, low = p % 2, p // 2
        self.at = {"x": d // 8, "y": d % 4, "z": ((d // 4) % 2) * 2 + low}
        self.side = low
        self.turn = {axis: [(self.at[axis] + k) % 4 for k in range(4)] for axis in "xyz"}
        self.near = {
            axis: [self.device(self.core, {**self.at, axis: self.turn[axis][k]}) for k in range(4)] for axis in "xyz"
        }
        self.twin = self.device(1 - self.core, self.at)
        z = self.at["z"]
        home = z + 1 - 2 * (z % 2)
        mate = home + self.core * (3 - z - home)
        self.out = self.device(self.core, {**self.at, "z": mate + self.side * (home - mate)})
        self.back = self.device(self.core, {**self.at, "z": home + self.side * (mate - home)})
        self.far = self.near["z"][2]

    def device(self, core, at):
        return {"pipe": (at["z"] % 2) * 2 + core, "dp": at["x"] * 8 + (at["z"] // 2) * 4 + at["y"]}

    def around(self, steps):
        return [self.near[axis][d] for axis in "xyz" for d in steps]


def send(src, dst, sems, i, device):
    copy = pltpu.make_async_remote_copy(
        src_ref=src, dst_ref=dst, send_sem=sems.at[0, i], recv_sem=sems.at[1, i],
        device_id=device, device_id_type=pl.DeviceIdType.MESH,
    )
    copy.start()
    return copy


def phase_buffers(size, relay, wide):
    quarter, small = size // 8, size // 32
    full = quarter if wide else small
    shapes = [("core", (3, size // 2, 128)), ("three", (3, 4, full, 128))]
    if relay:
        shapes += [("one", (3, 2, quarter // 2, 128)), ("two", (3, 2, quarter, 128))]
    else:
        shapes += [("one", (3, 3, quarter, 128))]
    shapes += [("wide", (3, 4, quarter, 128)) if wide else ("small", (3, 3, small, 128))]
    return shapes


def reduce_phase(me, g, phase, recv, sems, free):
    base, size, relay, wide = phase
    half, quarter, small = size // 2, size // 8, size // 32
    mine, others = base + me.core * half, base + (1 - me.core) * half
    step = [0]

    def go(src, dst, device):
        send(src, dst, sems, step[0], device)

    def wait(all_of_it):
        pltpu.make_async_remote_copy(
            src_ref=all_of_it, dst_ref=all_of_it, send_sem=sems.at[0, step[0]], recv_sem=sems.at[1, step[0]],
            device_id=me.twin, device_id_type=pl.DeviceIdType.MESH,
        ).wait()
        step[0] += 1

    def rows_of(c, start, count):
        return g.at[c, pl.ds(start, count), :]

    def release(i, devices):
        for device in devices:
            pl.semaphore_signal(free.at[i], inc=1, device_id=device, device_id_type=pl.DeviceIdType.MESH)

    def add(c, start, count, terms):
        own = pl.ds(start, count)
        value = g[c, own, :].astype(f32)
        for term in terms:
            value = value + term.astype(f32)
        g[c, own, :] = value.astype(bf16)

    def exchange(starts, rows, buf, turn):
        for c in range(3):
            buf[c, me.at[ORDERS[c][turn]]] = g[c, pl.ds(starts[c], rows), :]
        for d in (2, 1, 3):
            for c in range(3):
                block = buf.at[c, me.at[ORDERS[c][turn]]]
                go(block, block, me.near[ORDERS[c][turn]][d])

    def total_of(starts, rows, buf):
        for c in range(3):
            value = buf[c, 0].astype(f32)
            for j in range(1, 4):
                value = value + buf[c, j].astype(f32)
            g[c, pl.ds(starts[c], rows), :] = value.astype(bf16)

    go(g.at[:, pl.ds(others, half), :], recv.core, me.twin)
    yield
    wait(recv.core)
    release(0, [me.twin])
    for c in range(3):
        add(c, mine, half, [recv.core[c]])

    axes = [order[0] for order in ORDERS]
    chunk = [[mine + me.turn[axes[c]][k] * quarter for k in range(4)] for c in range(3)]
    one = [chunk[c][0] for c in range(3)]
    if relay:
        part = quarter // 2
        for c in range(3):
            go(rows_of(c, chunk[c][2], part), recv.one.at[c, 0], me.near[axes[c]][1])
            go(rows_of(c, chunk[c][2] + part, part), recv.one.at[c, 1], me.near[axes[c]][3])
        yield
        wait(recv.one)
        for c in range(3):
            add(c, chunk[c][1], part, [recv.one[c, 0]])
            add(c, chunk[c][3] + part, part, [recv.one[c, 1]])
            go(rows_of(c, chunk[c][1], quarter), recv.two.at[c, 0], me.near[axes[c]][1])
            go(rows_of(c, chunk[c][3], quarter), recv.two.at[c, 1], me.near[axes[c]][3])
        yield
        wait(recv.two)
        for c in range(3):
            add(c, one[c], quarter, [recv.two[c, 0], recv.two[c, 1]])
    else:
        for d in (2, 1, 3):
            for c in range(3):
                go(rows_of(c, chunk[c][d], quarter), recv.one.at[c, d - 1], me.near[axes[c]][d])
        yield
        wait(recv.one)
        for c in range(3):
            add(c, one[c], quarter, [recv.one[c, d] for d in range(3)])

    if wide:
        release(1, me.around((1, 2, 3)))
        exchange(one, quarter, recv.wide, 1)
        yield
        wait(recv.wide.at[:, 0:3])
        total_of(one, quarter, recv.wide)
        exchange(one, quarter, recv.three, 2)
        yield
        wait(recv.three.at[:, 0:3])
        total_of(one, quarter, recv.three)
    else:
        axes2 = [order[1] for order in ORDERS]
        two = [one[c] + me.at[axes2[c]] * small for c in range(3)]
        for d in (2, 1, 3):
            for c in range(3):
                block = rows_of(c, one[c] + me.turn[axes2[c]][d] * small, small)
                go(block, recv.small.at[c, d - 1], me.near[axes2[c]][d])
        yield
        wait(recv.small)
        release(1, me.around((1, 2, 3)))
        for c in range(3):
            add(c, two[c], small, [recv.small[c, d] for d in range(3)])
        exchange(two, small, recv.three, 2)
        yield
        wait(recv.three.at[:, 0:3])
        total_of(two, small, recv.three)
        pl.semaphore_wait(free.at[1], 9)
        for d in (2, 1, 3):
            for c in range(3):
                block = rows_of(c, two[c], small)
                go(block, block, me.near[axes2[c]][d])
        yield
        wait(recv.small)

    if wide:
        pl.semaphore_wait(free.at[1], 9)
    for d in (1, 3) if relay else (2, 1, 3):
        for c in range(3):
            block = rows_of(c, one[c], quarter)
            go(block, block, me.near[axes[c]][d])
    yield
    wait(recv.two if relay else recv.one)
    if relay:
        for c in range(3):
            block = rows_of(c, chunk[c][3], part)
            go(block, block, me.near[axes[c]][1])
            block = rows_of(c, chunk[c][1] + part, part)
            go(block, block, me.near[axes[c]][3])
        yield
        wait(recv.one)
    pl.semaphore_wait(free.at[0], 1)
    block = g.at[:, pl.ds(mine, half), :]
    go(block, block, me.twin)
    yield
    wait(recv.core)


def slot_kernel(names, *refs):
    r = Refs()
    for name, ref in zip(names, refs):
        setattr(r, name, ref)
    me = Where()
    first = me.side == 0
    loads = {}
    for i, (name, _) in enumerate(WEIGHTS):
        loads[name] = pltpu.make_async_copy(getattr(r, "h_" + name), getattr(r, name), r.loads.at[i])
        loads[name].start()
    barrier = pltpu.get_barrier_semaphore()
    friends = [me.twin] + me.around((1, 2, 3))
    for device in friends:
        pl.semaphore_signal(barrier, inc=1, device_id=device, device_id_type=pl.DeviceIdType.MESH)
    lane = lax.broadcasted_iota(jnp.int32, (8, 128), 1)
    counts = jnp.zeros((8, 128), jnp.int32)
    for c in range(CLIPS):
        counts = jnp.where(lane == c, r.frames[0, 1, me.core, c], counts)
    r.counts[...] = counts
    pl.semaphore_wait(barrier, len(friends))
    told = send(r.counts, r.far_counts, r.swaps, 4, me.far)
    swap = send(r.local.at[1 - me.side], r.arrived, r.swaps, 0, me.out)
    away = me.side * me.core == 1
    lookup = pltpu.make_async_copy(r.far_counts, r.scalars, r.loads.at[len(WEIGHTS)])

    @pl.when(away)
    def _():
        told.wait_recv()
        lookup.start()
        lookup.wait()

    @pl.when(jnp.logical_not(away))
    def _():
        for c in range(CLIPS):
            r.scalars[0, c] = r.frames[0, me.side, me.core, c]

    source, label, live = unit_order([r.scalars[0, c] for c in range(CLIPS)])
    fill_mask(r.mask, label)
    fill_order(r.order, source)
    enc, pred = Refs(), Refs()
    enc.vec = columns(r.eg[...], r.eb[...], r.exb[...])
    pred.vec = columns(r.pg[...], r.pb[...], r.pxb[...])
    enc.project, enc.merge, enc.expand, enc.reduce = r.ew, r.em, r.ex, r.er
    pred.project, pred.merge, pred.expand, pred.reduce = r.pw, r.pm, r.px, r.pr
    es, ps = Refs(), Refs()
    for name, _, _ in KEPT:
        setattr(es, name, getattr(r, "e_" + name))
        setattr(ps, name, getattr(r, "p_" + name))
    for name, _, _ in SHARED:
        setattr(es, name, getattr(r, name))
        setattr(ps, name, getattr(r, name))
    es.e, es.over, ps.e, ps.over = r.e_e, r.e_over, r.p_e, r.p_over


    @pl.when(jnp.logical_not(first))
    def _():
        swap.wait_recv()

    far_rows = pltpu.make_async_remote_copy(
        src_ref=r.local.at[1], dst_ref=r.cotangent, send_sem=r.swaps.at[0, 2], recv_sem=r.swaps.at[1, 2],
        device_id=me.far, device_id_type=pl.DeviceIdType.MESH,
    )

    @pl.when(away)
    def _():
        far_rows.start()

    @pl.when(first)
    def _():
        r.x[...] = r.local[0]

    @pl.when(jnp.logical_not(first))
    def _():
        r.x[...] = r.arrived[...]

    r.stream[...] = dot(r.x[...], r.order[...], 0, 0)
    for copy in loads.values():
        copy.wait()

    block_forward(r.stream, r.stream2, enc, es, HEADS, r.mask)
    r.sent[...] = r.stream2[...].astype(bf16)
    r.stream[...] = dot(r.embed[...], r.sent[...], 0, 0) + r.embed_bias[...].astype(f32).reshape(1, F).T
    block_forward(r.stream, r.stream2, pred, ps, PHEADS, r.mask)

    alive = lax.broadcasted_iota(jnp.int32, (F, ROWS), 1) < live
    r.out[...] = dot(r.order[...], jnp.where(alive, r.stream2[...], 0.0).astype(bf16), 1, 1).astype(bf16)
    copy_out = pltpu.make_async_remote_copy(
        src_ref=r.sends, dst_ref=r.back, send_sem=r.swaps.at[0, 1], recv_sem=r.swaps.at[1, 1],
        device_id=me.back, device_id_type=pl.DeviceIdType.MESH,
    )
    far_out = pltpu.make_async_remote_copy(
        src_ref=r.out, dst_ref=r.kept, send_sem=r.swaps.at[0, 3], recv_sem=r.swaps.at[1, 3],
        device_id=me.far, device_id_type=pl.DeviceIdType.MESH,
    )

    @pl.when(first)
    def _():
        r.sends[...] = r.out[...]
        copy_out.start()
        swap.wait_recv()
        r.cotangent[...] = r.arrived[...]

    @pl.when(away)
    def _():
        far_out.start()
        far_rows.wait()

    @pl.when(me.side * (1 - me.core) == 1)
    def _():
        r.cotangent[...] = r.local[1]
        r.kept[...] = r.out[...]

    swap.wait_send()
    told.wait_send()

    @pl.when(jnp.logical_not(away))
    def _():
        told.wait_recv()

    cotangent = r.cotangent[...]
    r.stream[...] = jnp.where(alive, dot(cotangent, r.order[...], 0, 0), 0.0)

    g = r.grads
    phases = []
    for i, phase in enumerate(PHASES):
        recv = Refs()
        for name, _ in phase_buffers(*phase[1:]):
            setattr(recv, name, getattr(r, f"{name}{i}"))
        phases.append(reduce_phase(me, g, phase, recv, r.sems.at[i], r.free.at[i]))

    ticks = iter(PLAN)

    def tick():
        for i in next(ticks):
            next(phases[i], None)

    sums = block_backward(r.stream, pred, ps, PHEADS, g, PRED_AT, tick)
    r.q[...] = r.stream[...].astype(bf16)
    de = r.q[...]
    place(g, PRED_AT["embed"], dot(r.sent[...], de, 1, 1))
    place_sums(g, PRED_AT["small"], sums + [total(de)])
    g[:, PRED_AT["end"] : ENC_AT["reduce"], :] = jnp.zeros((3, ENC_AT["reduce"] - PRED_AT["end"], 128), bf16)
    g[:, ENC_AT["gap"] : ENC_AT["project"], :] = jnp.zeros((3, ENC_AT["project"] - ENC_AT["gap"], 128), bf16)
    g[:, ENC_AT["end"] : TOTAL, :] = jnp.zeros((3, TOTAL - ENC_AT["end"], 128), bf16)
    r.stream[...] = dot(r.embed[...], de, 1, 0).astype(bf16).astype(f32)
    tick()
    sums = block_backward(r.stream, enc, es, HEADS, g, ENC_AT, tick)
    place_sums(g, ENC_AT["small"], sums)
    tick()
    dx = dot(r.order[...], r.stream[...].astype(bf16), 1, 1).astype(bf16)

    @pl.when(first)
    def _():
        r.kept[...] = dx

    @pl.when(jnp.logical_not(first))
    def _():
        r.sends[...] = dx

    for i in TAIL:
        if i is None:

            @pl.when(jnp.logical_not(first))
            def _():
                copy_out.start()

        else:
            next(phases[i], None)
    copy_out.wait()

    @pl.when(away)
    def _():
        far_out.wait()


PLAN = (
    (), (), (), (), (0,), (), (), (), (), (), (), (), (0,), (1,), (), (), (), (1, 0, 2,), (), (1, 2, 3,), (0,), (), (), (3, 1,), (4,),
)
TAIL = (2, 0, 4, 3, 1, 2, 0, 4, 3, 1, 2, 0, 4, 3, 1, 2, 0, 4, 3, 1, 2, 0, 4, None, 2, 3, 1, 0, 4, 3, 1, 4)


def slot_call(frames, local, weights):
    args = [("frames", frames), ("local", local)]
    big = {name for name, _ in WEIGHTS}
    order = ("eg", "eb", "ew", "em", "ex", "exb", "er", "embed", "embed_bias", "pg", "pb", "pw", "pm", "px", "pxb", "pr")
    specs = [pl.BlockSpec(memory_space=pltpu.SMEM), pl.BlockSpec(memory_space=pltpu.VMEM)]
    for name, weight in zip(order, weights):
        args.append(("h_" + name if name in big else name, weight))
        specs.append(pl.BlockSpec(memory_space=pl.ANY if name in big else pltpu.VMEM))
    outs = [("grads", (3, TOTAL, 128), bf16), ("kept", (ROWS, F), bf16), ("back", (ROWS, F), bf16)]
    scratch = [
        ("mask", (BLOCKS, BLOCK, BLOCK), f32), ("order", (ROWS, ROWS), bf16), ("out", (ROWS, F), bf16),
        ("stream", (F, ROWS), f32), ("stream2", (F, ROWS), f32), ("sent", (F, ROWS), bf16),
        ("arrived", (ROWS, F), bf16), ("cotangent", (ROWS, F), bf16), ("x", (ROWS, F), bf16),
        ("counts", (8, 128), jnp.int32), ("far_counts", (8, 128), jnp.int32), ("sends", (ROWS, F), bf16),
        ("e_e", (HEADS, BLOCKS, BLOCK, BLOCK), bf16), ("p_e", (PHEADS, BLOCKS, BLOCK, BLOCK), bf16),
        ("e_over", (8, ROWS), f32), ("p_over", (16, ROWS), f32),
    ]
    scratch += [(n, sh, bf16) for n, sh in WEIGHTS]
    scratch += [("e_" + n, sh, d) for n, sh, d in KEPT] + [("p_" + n, sh, d) for n, sh, d in KEPT]
    scratch += list(SHARED)
    for i, phase in enumerate(PHASES):
        scratch += [(f"{name}{i}", shape, bf16) for name, shape in phase_buffers(*phase[1:])]
    sems = [("loads", (len(WEIGHTS) + 1,)), ("swaps", (2, 5)), ("sems", (len(PHASES), 2, 9))]
    names = [n for n, _ in args] + [n for n, _, _ in outs] + [n for n, _, _ in scratch] + [n for n, _ in sems] + ["free", "scalars"]
    return pl.pallas_call(
        functools.partial(slot_kernel, names),
        out_shape=[pltpu.VMEM(sh, d) for _, sh, d in outs],
        in_specs=specs,
        out_specs=[pl.BlockSpec(memory_space=pltpu.VMEM)] * len(outs),
        scratch_shapes=[pltpu.VMEM(sh, d) for _, sh, d in scratch] + [pltpu.SemaphoreType.DMA(sh) for _, sh in sems]
        + [pltpu.SemaphoreType.REGULAR((len(PHASES), 2)), pltpu.SMEM((8, 128), jnp.int32)],
        compiler_params=pltpu.CompilerParams(
            vmem_limit_bytes=52 * 2**20, collective_id=0, has_side_effects=True
        ),
    )(*[a for _, a in args])


LAYERS = (("pg", "pb", "pw", "pm", "px", "pxb", "pr"), ("eg", "eb", "ew", "em", "ex", "exb", "er"))
BIG = {"w": (F, 3 * F), "m": (F, F), "x": (F, FF), "r": (FF, F)}


def widen(g_ref, at, out_ref, rows, col):
    for c in range(3):
        out_ref[rows, col + c * 128 : col + c * 128 + 128] = g_ref[c, at : at + F, :].astype(f32)


def unpack_kernel(names, *refs):
    r = Refs()
    for name, ref in zip(names, refs):
        setattr(r, name, ref)
    copies = []

    def ship(src, dst):
        copy = pltpu.make_async_copy(src, dst, r.sems.at[len(copies)])
        copy.start()
        copies.append(copy)

    side = lax.axis_index("pipe") // 2
    r.wide[0] = r.kept[...].astype(f32)
    ship(r.wide.at[0], r.result.at[side])
    r.wide[1] = r.back[...].astype(f32)
    ship(r.wide.at[1], r.result.at[1 - side])
    g = r.grads
    for layer, at in (("p", PRED_AT), ("e", ENC_AT)):
        for part in range(4):
            rows = slice(part * F, part * F + F)
            widen(g, at["reduce"] + part * F, getattr(r, "s_" + layer + "r"), rows, 0)
        ship(getattr(r, "s_" + layer + "r"), getattr(r, layer + "r"))
        for part in range(4):
            widen(g, at["expand"] + part * F, getattr(r, "s_" + layer + "x"), slice(0, F), part * F)
        ship(getattr(r, "s_" + layer + "x"), getattr(r, layer + "x"))
        for part in range(3):
            widen(g, at["project"] + part * F, getattr(r, "s_" + layer + "w"), slice(0, F), part * F)
        ship(getattr(r, "s_" + layer + "w"), getattr(r, layer + "w"))
        widen(g, at["merge"], getattr(r, "s_" + layer + "m"), slice(0, F), 0)
        ship(getattr(r, "s_" + layer + "m"), getattr(r, layer + "m"))
        if layer == "p":
            widen(g, at["embed"], r.s_embed, slice(0, F), 0)
            ship(r.s_embed, r.embed)
        small = at["small"]
        rows = jnp.concatenate([g[c, small : small + 16, :] for c in range(3)], axis=1).astype(f32)
        getattr(r, layer + "g")[...] = rows[0:2]
        getattr(r, layer + "b")[...] = rows[2:8]
        for part in range(4):
            getattr(r, layer + "xb")[part * F : part * F + F] = rows[8 + part]
        if layer == "p":
            r.embed_bias[...] = rows[12]
    for copy in copies:
        copy.wait()


def unpack_call(grads, kept, back):
    big = [("embed", (F, F))] + [(layer + n, BIG[n]) for layer in "pe" for n in BIG]
    small = [("embed_bias", (F,))]
    for layer in "pe":
        small += [(layer + "g", (2, F)), (layer + "b", (6, F)), (layer + "xb", (FF,))]
    outs = [("result", (2, ROWS, F))] + big + small
    names = ["grads", "kept", "back"] + [n for n, _ in outs] + ["s_" + n for n, _ in big] + ["wide", "sems"]
    values = pl.pallas_call(
        functools.partial(unpack_kernel, names),
        out_shape=[jax.ShapeDtypeStruct(sh, f32) for _, sh in outs],
        in_specs=[pl.BlockSpec(memory_space=pltpu.VMEM)] * 3,
        out_specs=[pl.BlockSpec(memory_space=pl.ANY)] * (1 + len(big))
        + [pl.BlockSpec(memory_space=pltpu.VMEM)] * len(small),
        scratch_shapes=[pltpu.VMEM(sh, f32) for _, sh in big]
        + [pltpu.VMEM((2, ROWS, F), f32), pltpu.SemaphoreType.DMA((len(big) + 2,))],
        compiler_params=pltpu.CompilerParams(vmem_limit_bytes=24 * 2**20),
    )(*[pltpu.with_memory_space_constraint(v, pltpu.VMEM) for v in (grads, kept, back)])
    return dict(zip([n for n, _ in outs], values))


def body(segment_data, clip_frames, *weights):
    g = unpack_call(*slot_call(clip_frames, segment_data[0, 0], weights))
    order = ("eg", "eb", "ew", "em", "ex", "exb", "er", "embed", "embed_bias", "pg", "pb", "pw", "pm", "px", "pxb", "pr")
    return (g["result"][None, None],) + tuple(g[n] for n in order)


def solution(mesh):
    return jax.shard_map(
        body,
        mesh=mesh,
        in_specs=(P("pipe", "dp", None, None, None), P("dp", None, None, None)) + (P(),) * 16,
        out_specs=(P("pipe", "dp", None, None, None),) + (P(),) * 16,
        check_vma=False,
    )
```

profile of v0, /device:TPU:1, one launch (start us, length us, event | category | flops | bytes accessed | tf_op | source)
XLA Modules:
  0.0 89.9 jit_solution(280108790644749360)
XLA Ops:
  0.7 82.5 %shard_map.305 = (bf16[3,10240,128]{2,1,0:T(8,128)(2,1)S(1)}, bf16[512,384]{1,0:T(8,128)(2,1)S(1)}, bf16[512,384]{1,0:T(8,128)(2,1)S(1)}) custom-call(s32[1,2,2,8]{3,2,1,0:T(2,128)} %refs_0_.1, bf16[2,512,384]{2,1,0:T(8,128)(2,1)} %bitcast.2, bf16[2,384]{1,0:T(2,128)(2,1)} %refs_2_.1, bf16[6,384]{1,0:T(8,128)(2,1)} %refs_3_.1, bf16[384,1152]{1,0:T(8,128)(2,1)} %refs_4_.1, ...), custom_call_target="tpu_custom_call" | custom-call | tf_op jit(solution)/shard_map/pallas_call | solution.py:671
  83.2 6.5 %shard_map.306 = (f32[2,512,384]{2,1,0:T(8,128)}, f32[384,384]{1,0:T(8,128)}, f32[384,1152]{1,0:T(8,128)}, f32[384,384]{1,0:T(8,128)}, f32[384,1536]{1,0:T(8,128...) custom-call(bf16[3,10240,128]{2,1,0:T(8,128)(2,1)S(1)} %get-tuple-el, ...), custom_call_target="tpu_custom_call" | custom-call | tf_op jit(solution)/shard_map/pallas_call | solution.py:745
where the time goes:
time: 90 us; the launch traced here: 89.9 us
  Pallas kernels  89 us (99%)
    pallas_call x1, Pallas kernels, slot_call(): pl.pallas_call(functools.partial(slot_kernel, names), out_shape=[pltpu.VM...  82.5 us
    pallas_call x1, Pallas kernels, unpack_call(): pl.pallas_call(functools.partial(unpack_kernel, names), out_shape=[jax.Sh...  6.5 us

commit v1 on v0

--- a/solution.py
+++ b/solution.py
@@ -167,7 +167,7 @@
     return jnp.sum(x.astype(f32), axis=1, keepdims=True)
 
 
-def block_backward(grad_ref, w, s, heads, g_ref, at, tick):
+def block_backward(grad_ref, w, s, heads, g_ref, at, tick, late):
     size = F // heads
     vec = w.vec
     sums = [None] * 12
@@ -229,15 +229,20 @@
     sums[4] = total(s.dz[2 * F : 3 * F, :])
     da = dot(w.project[...], s.dz[...], 1, 0)
     s.t[...] = da
-    for t in range(ROWS // 128):
+
+    def last(t):
         cols = slice(t * 128, t * 128 + 128)
         grad_ref[:, cols] += norm_back(s.t[:, cols] * vec[:, 0:1], s.n1[:, cols], s.i1[:, cols])
+
+    for t in range(ROWS // 128):
+        if not late:
+            last(t)
         if t < 3:
             place(g_ref, at["project"] + t * F, dot(s.a1[...], s.dz[t * F : t * F + F, :], 1, 1))
     sums[0] = total(s.t[...] * s.n1[...])
     sums[2] = total(s.t[...])
     tick()
-    return sums
+    return sums, last
 
 
 def columns(gains, biases, hidden):
@@ -599,7 +604,7 @@
         for i in next(ticks):
             next(phases[i], None)
 
-    sums = block_backward(r.stream, pred, ps, PHEADS, g, PRED_AT, tick)
+    sums, _ = block_backward(r.stream, pred, ps, PHEADS, g, PRED_AT, tick, False)
     r.q[...] = r.stream[...].astype(bf16)
     de = r.q[...]
     place(g, PRED_AT["embed"], dot(r.sent[...], de, 1, 1))
@@ -609,20 +614,23 @@
     g[:, ENC_AT["end"] : TOTAL, :] = jnp.zeros((3, TOTAL - ENC_AT["end"], 128), bf16)
     r.stream[...] = dot(r.embed[...], de, 1, 0).astype(bf16).astype(f32)
     tick()
-    sums = block_backward(r.stream, enc, es, HEADS, g, ENC_AT, tick)
+    sums, last = block_backward(r.stream, enc, es, HEADS, g, ENC_AT, tick, True)
     place_sums(g, ENC_AT["small"], sums)
     tick()
-    dx = dot(r.order[...], r.stream[...].astype(bf16), 1, 1).astype(bf16)
-
-    @pl.when(first)
-    def _():
-        r.kept[...] = dx
-
-    @pl.when(jnp.logical_not(first))
-    def _():
-        r.sends[...] = dx
-
-    for i in TAIL:
+    for n, i in enumerate(TAIL):
+        if n == 3:
+            for t in range(ROWS // 128):
+                last(t)
+            dx = dot(r.order[...], r.stream[...].astype(bf16), 1, 1).astype(bf16)
+
+            @pl.when(first)
+            def _():
+                r.kept[...] = dx
+
+            @pl.when(jnp.logical_not(first))
+            def _():
+                r.sends[...] = dx
+
         if i is None:
 
             @pl.when(jnp.logical_not(first))

time: 90 us -> 89.5 us (level)
  no operation moved by 1% of the time
where the time goes in v1:
time: 89.5 us; the launch traced here: 89.3 us
  Pallas kernels  88.5 us (99%)
    pallas_call x1, Pallas kernels, slot_call(): pl.pallas_call(functools.partial(slot_kernel, names), out_shape=[pltpu.VM...  82 us
    pallas_call x1, Pallas kernels, unpack_call(): pl.pallas_call(functools.partial(unpack_kernel, names), out_shape=[jax.Sh...  6.5 us

profile of v1, /device:TPU:1, one launch (start us, length us, event | category | flops | bytes accessed | tf_op | source)
XLA Modules:
  0.0 89.3 jit_solution(4906205279123232028)
XLA Ops:
  0.7 82.0 %shard_map.305 = (bf16[3,10240,128]{2,1,0:T(8,128)(2,1)S(1)}, bf16[512,384]{1,0:T(8,128)(2,1)S(1)}, bf16[512,384]{1,0:T(8,128)(2,1)S(1)}) custom-call(s32[1,2,2,8]{3,2,1,0:T(2,128)} %refs_0_.1, bf16[2,512,384]{2,1,0:T(8,128)(2,1)} %bitcast.2, bf16[2,384]{1,0:T(2,128)(2,1)} %refs_2_.1, bf16[6,384]{1,0:T(8,128)(2,1)} %refs_3_.1, bf16[384,1152]{1,0:T(8,128)(2,1)} %refs_4_.1, ...), custom_call_target="tpu_custom_call" | custom-call | tf_op jit(solution)/shard_map/pallas_call | solution.py:679
  82.7 6.5 %shard_map.306 = (f32[2,512,384]{2,1,0:T(8,128)}, f32[384,384]{1,0:T(8,128)}, f32[384,1152]{1,0:T(8,128)}, f32[384,384]{1,0:T(8,128)}, f32[384,1536]{1,0:T(8,128...) custom-call(bf16[3,10240,128]{2,1,0:T(8,128)(2,1)S(1)} %get-tuple-el, ...), custom_call_target="tpu_custom_call" | custom-call | tf_op jit(solution)/shard_map/pallas_call | solution.py:753

commit v2 on v1

--- a/solution.py
+++ b/solution.py
@@ -361,11 +361,12 @@
             value = value + term.astype(f32)
         g[c, own, :] = value.astype(bf16)
 
-    def exchange(starts, rows, buf, turn):
+    def exchange(starts, rows, buf, turn, came):
         for c in range(3):
+            if came[c]:
+                add(c, starts[c], rows, [term[...] for term in came[c]])
             buf[c, me.at[ORDERS[c][turn]]] = g[c, pl.ds(starts[c], rows), :]
-        for d in (2, 1, 3):
-            for c in range(3):
+            for d in (2, 1, 3):
                 block = buf.at[c, me.at[ORDERS[c][turn]]]
                 go(block, block, me.near[ORDERS[c][turn]][d])
 
@@ -379,18 +380,16 @@
     go(g.at[:, pl.ds(others, half), :], recv.core, me.twin)
     yield
     wait(recv.core)
-    release(0, [me.twin])
-    for c in range(3):
-        add(c, mine, half, [recv.core[c]])
-
     axes = [order[0] for order in ORDERS]
     chunk = [[mine + me.turn[axes[c]][k] * quarter for k in range(4)] for c in range(3)]
     one = [chunk[c][0] for c in range(3)]
     if relay:
         part = quarter // 2
         for c in range(3):
+            add(c, mine, half, [recv.core[c]])
             go(rows_of(c, chunk[c][2], part), recv.one.at[c, 0], me.near[axes[c]][1])
             go(rows_of(c, chunk[c][2] + part, part), recv.one.at[c, 1], me.near[axes[c]][3])
+        release(0, [me.twin])
         yield
         wait(recv.one)
         for c in range(3):
@@ -400,40 +399,39 @@
             go(rows_of(c, chunk[c][3], quarter), recv.two.at[c, 1], me.near[axes[c]][3])
         yield
         wait(recv.two)
+        came = [[recv.two.at[c, k] for k in range(2)] for c in range(3)]
+    else:
         for c in range(3):
-            add(c, one[c], quarter, [recv.two[c, 0], recv.two[c, 1]])
-    else:
-        for d in (2, 1, 3):
-            for c in range(3):
+            add(c, mine, half, [recv.core[c]])
+            for d in (2, 1, 3):
                 go(rows_of(c, chunk[c][d], quarter), recv.one.at[c, d - 1], me.near[axes[c]][d])
+        release(0, [me.twin])
         yield
         wait(recv.one)
-        for c in range(3):
-            add(c, one[c], quarter, [recv.one[c, d] for d in range(3)])
+        came = [[recv.one.at[c, k] for k in range(3)] for c in range(3)]
 
     if wide:
+        exchange(one, quarter, recv.wide, 1, came)
         release(1, me.around((1, 2, 3)))
-        exchange(one, quarter, recv.wide, 1)
         yield
         wait(recv.wide.at[:, 0:3])
         total_of(one, quarter, recv.wide)
-        exchange(one, quarter, recv.three, 2)
+        exchange(one, quarter, recv.three, 2, [[]] * 3)
         yield
         wait(recv.three.at[:, 0:3])
         total_of(one, quarter, recv.three)
     else:
         axes2 = [order[1] for order in ORDERS]
         two = [one[c] + me.at[axes2[c]] * small for c in range(3)]
-        for d in (2, 1, 3):
-            for c in range(3):
+        for c in range(3):
+            add(c, one[c], quarter, [term[...] for term in came[c]])
+            for d in (2, 1, 3):
                 block = rows_of(c, one[c] + me.turn[axes2[c]][d] * small, small)
                 go(block, recv.small.at[c, d - 1], me.near[axes2[c]][d])
         yield
         wait(recv.small)
+        exchange(two, small, recv.three, 2, [[recv.small.at[c, d] for d in range(3)] for c in range(3)])
         release(1, me.around((1, 2, 3)))
-        for c in range(3):
-            add(c, two[c], small, [recv.small[c, d] for d in range(3)])
-        exchange(two, small, recv.three, 2)
         yield
         wait(recv.three.at[:, 0:3])
         total_of(two, small, recv.three)

time: 89.5 us -> 89.2 us (level)
  no operation moved by 1% of the time
where the time goes in v2:
time: 89.2 us; the launch traced here: 89.1 us
  Pallas kernels  88.2 us (99%)
    pallas_call x1, Pallas kernels, slot_call(): pl.pallas_call(functools.partial(slot_kernel, names), out_shape=[pltpu.VM...  81.7 us
    pallas_call x1, Pallas kernels, unpack_call(): pl.pallas_call(functools.partial(unpack_kernel, names), out_shape=[jax.Sh...  6.5 us

profile of v2, /device:TPU:1, one launch (start us, length us, event | category | flops | bytes accessed | tf_op | source)
XLA Modules:
  0.0 89.1 jit_solution(13864737153740718388)
XLA Ops:
  0.7 81.7 %shard_map.305 = (bf16[3,10240,128]{2,1,0:T(8,128)(2,1)S(1)}, bf16[512,384]{1,0:T(8,128)(2,1)S(1)}, bf16[512,384]{1,0:T(8,128)(2,1)S(1)}) custom-call(s32[1,2,2,8]{3,2,1,0:T(2,128)} %refs_0_.1, bf16[2,512,384]{2,1,0:T(8,128)(2,1)} %bitcast.2, bf16[2,384]{1,0:T(2,128)(2,1)} %refs_2_.1, bf16[6,384]{1,0:T(8,128)(2,1)} %refs_3_.1, bf16[384,1152]{1,0:T(8,128)(2,1)} %refs_4_.1, ...), custom_call_target="tpu_custom_call" | custom-call | tf_op jit(solution)/shard_map/pallas_call | solution.py:677
  82.4 6.5 %shard_map.306 = (f32[2,512,384]{2,1,0:T(8,128)}, f32[384,384]{1,0:T(8,128)}, f32[384,1152]{1,0:T(8,128)}, f32[384,384]{1,0:T(8,128)}, f32[384,1536]{1,0:T(8,128...) custom-call(bf16[3,10240,128]{2,1,0:T(8,128)(2,1)S(1)} %get-tuple-el, ...), custom_call_target="tpu_custom_call" | custom-call | tf_op jit(solution)/shard_map/pallas_call | solution.py:751
